TPU v7x, 128 devices: a whole 4x4x4 slice. The times are simulated.
128 devices in a mesh: dp: 8 (over y, core), expert: 16 (over x, z).
Axes of the slice: x: 4, y: 4, z: 4, core: 2. Of those that a mesh axis runs over, the one named last changes fastest.
Arguments:
- tokens: bfloat16 [16384, 4096], P(('dp', 'expert')), may hold values from -6 to 6
- out_grad: bfloat16 [16384, 4096], P(('dp', 'expert')), may hold values from -6 to 6
- group_token: int32 [128, 16, 32], P(('dp', 'expert')), may hold values from 0 to 127, as said below
- group_count: int32 [128, 16], P(('dp', 'expert')), may hold values from 1 to 32, as said below
- group_prob: bfloat16 [128, 16, 32], P(('dp', 'expert')), may hold values from 0.049804688 to 1
- w_gate: bfloat16 [16, 4096, 768], P('expert'), may hold values from -0.09375 to 0.09375
- w_up: bfloat16 [16, 4096, 768], P('expert'), may hold values from -0.09375 to 0.09375
- w_down: bfloat16 [16, 768, 4096], P('expert'), may hold values from -0.21875 to 0.21875
Outputs:
- token_grad: bfloat16 [16384, 4096], P(('dp', 'expert'))
- route_grad: bfloat16 [128, 16, 32], P(('dp', 'expert'))
- grad_gate: bfloat16 [16, 4096, 768], P('expert', 'dp')
- grad_up: bfloat16 [16, 4096, 768], P('expert', 'dp')
- grad_down: bfloat16 [16, 768, 4096], P('expert', None, 'dp')
Inputs may be any that keep to these rules, and one draw needn't show every extreme that they name: `group_token`: within one group (s, e) the 32 entries name distinct tokens of device s; entries of slots that are not live are arbitrary. `group_count`: in every draw some expert's group is full from every device, and every device has a full group.
All inputs are finite; a program needn't handle non-finite values.
Results may differ from a plain program's by a relative error of at most 0.018.
Values may be sent and summed in bfloat16 or wider, within the bound.
A program may use at most 128 MiB of HBM per device.

v0:
```python
import jax
import jax.numpy as jnp
from jax import lax
from jax.sharding import PartitionSpec as P


def contract_last(left, right):
    return lax.dot_general(
        left, right, (((1,), (1,)), ((), ())), preferred_element_type=jnp.float32
    )


def contract_first(left, right):
    return lax.dot_general(
        left, right, (((0,), (0,)), ((), ())), preferred_element_type=jnp.float32
    )


def shards(tokens, out_grad, group_token, group_count, group_prob, w_gate, w_up, w_down):
    experts = group_token.shape[1]
    capacity = group_token.shape[2]
    width = tokens.shape[1]
    tok_count = tokens.shape[0]
    zero_half = jnp.zeros((), jnp.bfloat16)
    tok_index = group_token[0]
    live_slot = lax.broadcasted_iota(jnp.int32, (experts, capacity), 1) < group_count[0][:, None]
    route_prob = jnp.where(live_slot, group_prob[0], zero_half)
    send_x = jnp.where(live_slot[..., None], tokens[tok_index], zero_half)
    send_dy = jnp.where(live_slot[..., None], out_grad[tok_index], zero_half)
    got_x = lax.all_to_all(send_x, "expert", split_axis=0, concat_axis=0, tiled=True)
    expert_rows = got_x.reshape(-1, width)
    weight_gate = w_gate[0]
    weight_up = w_up[0]
    weight_down = w_down[0]
    gate_pre = jnp.dot(expert_rows, weight_gate, preferred_element_type=jnp.float32)
    up_pre = jnp.dot(expert_rows, weight_up, preferred_element_type=jnp.float32)
    sigmoid_gate = jax.nn.sigmoid(gate_pre)
    activated = gate_pre * sigmoid_gate
    hidden = (activated * up_pre).astype(jnp.bfloat16)
    expert_out = jnp.dot(hidden, weight_down, preferred_element_type=jnp.float32).astype(
        jnp.bfloat16
    )
    returned = lax.all_to_all(
        expert_out.reshape(experts, capacity, width),
        "expert",
        split_axis=0,
        concat_axis=0,
        tiled=True,
    )
    got_dy, got_prob = (
        lax.all_to_all(send_dy, "expert", split_axis=0, concat_axis=0, tiled=True),
        lax.all_to_all(route_prob, "expert", split_axis=0, concat_axis=0, tiled=True),
    )
    grad_rows = got_dy.reshape(-1, width)
    prob_rows = got_prob.reshape(-1)
    output_grad = (prob_rows.astype(jnp.float32)[:, None] * grad_rows.astype(jnp.float32)).astype(
        jnp.bfloat16
    )
    hidden_grad = contract_last(output_grad, weight_down)
    gate_grad = (
        hidden_grad * up_pre * sigmoid_gate * (1.0 + gate_pre * (1.0 - sigmoid_gate))
    ).astype(jnp.bfloat16)
    up_grad = (hidden_grad * activated).astype(jnp.bfloat16)
    input_grad = (contract_last(gate_grad, weight_gate) + contract_last(up_grad, weight_up)).astype(
        jnp.bfloat16
    )
    input_grad = input_grad.reshape(experts, capacity, width)
    back_rows = lax.all_to_all(input_grad, "expert", split_axis=0, concat_axis=0, tiled=True)
    route_grad = jnp.sum(
        send_dy.astype(jnp.float32) * returned.astype(jnp.float32), axis=-1
    ).astype(jnp.bfloat16)
    part_gate = contract_first(expert_rows, gate_grad)
    part_up = contract_first(expert_rows, up_grad)
    part_down = contract_first(hidden, output_grad)
    summed_gate, summed_up, summed_down = (
        lax.psum_scatter(
            part_gate.astype(jnp.bfloat16), "dp", scatter_dimension=0, tiled=True
        ).astype(jnp.float32),
        lax.psum_scatter(
            part_up.astype(jnp.bfloat16), "dp", scatter_dimension=0, tiled=True
        ).astype(jnp.float32),
        lax.psum_scatter(
            part_down.astype(jnp.bfloat16), "dp", scatter_dimension=1, tiled=True
        ).astype(jnp.float32),
    )
    replicas = lax.axis_size("dp")
    grad_gate = (summed_gate / replicas).astype(jnp.bfloat16)[None]
    grad_up = (summed_up / replicas).astype(jnp.bfloat16)[None]
    grad_down = (summed_down / replicas).astype(jnp.bfloat16)[None]
    flat_index = tok_index.reshape(1, -1)
    token_ids = lax.broadcasted_iota(jnp.int32, (tok_count, 1), 0)
    selector = ((flat_index == token_ids) & live_slot.reshape(1, -1)).astype(jnp.bfloat16)
    token_grad = jnp.dot(
        selector, back_rows.reshape(-1, width), preferred_element_type=jnp.float32
    ).astype(jnp.bfloat16)
    return (token_grad, route_grad[None], grad_gate, grad_up, grad_down)


def solution(mesh):
    in_specs = (
        P(("dp", "expert"), None),
        P(("dp", "expert"), None),
        P(("dp", "expert"), None, None),
        P(("dp", "expert"), None),
        P(("dp", "expert"), None, None),
        P("expert", None, None),
        P("expert", None, None),
        P("expert", None, None),
    )
    out_specs = (
        P(("dp", "expert"), None),
        P(("dp", "expert"), None, None),
        P("expert", "dp", None),
        P("expert", "dp", None),
        P("expert", None, "dp"),
    )
    return jax.shard_map(shards, mesh=mesh, in_specs=in_specs, out_specs=out_specs, check_vma=False)
```

profile of v0, /device:TPU:1, one launch (start us, length us, event | category | flops | bytes accessed | tf_op | source)
XLA Modules:
  0.0 365.8 jit_solution(6783201654211264539)
XLA Ops:
  7.2 0.8 iota_compare_fusion.2
  8.0 0.7 compare_select_fusion
  8.8 4.4 %gather_fusion.1 = bf16[512,4096]{1,0:T(8,128)(2,1)} fusion(bf16[128,4096]{1,0:T(8,128)(2,1)S(1)} %copy-done, s32[1024]{0:T(1024)S(1)} %pad_clamp_fusion), kind=kCustom, calls=%fused_computation.1 | custom fusion | bytes 8390656 | tf_op jit(solution)/shard_map/gather | solution.py:28
  13.2 2.7 broadcast_select_fusion
  15.9 57.7 %all_to_all.26 = bf16[16,32,4096]{2,1,0:T(8,128)(2,1)S(1)} all-to-all(bf16[16,32,4096]{2,1,0:T(8,128)(2,1)S(1)} %broadcast_select_fusion), channel_id=1, replica_groups=mesh['dp'=8,'expert'=16] {'expert'}, dimensions={0} | all-to-all | bytes 8388608 | tf_op jit(solution)/shard_map/all_to_all | solution.py:30
  73.6 3.4 fusion.3
  77.1 4.6 %multiply_convert_fusion.4 = (bf16[512,768]{1,0:T(8,128)(2,1)S(1)}, f32[512,768]{1,0:T(8,128)}) fusion(f32[512,768]{1,0:T(8,128)S(1)} %fusion.3, bf16[512,4096]{1,0:T(8,128)(2,1)S(1)} %bitcast.68, bf16[1,4096,768]{2,1,0:T(8,128)(2,1)S(1)} %bitcast.80), kind=kOutput, calls=%fused_computation.29 | convolution fusion | flops 3223584768 | bytes 14417920 | tf_op jit(solution)/shard_map/dot_general | solution.py:36
  81.7 5.0 %fusion.13 = bf16[512,4096]{1,0:T(8,128)(2,1)} fusion(bf16[512,768]{1,0:T(8,128)(2,1)S(1)} %get-tuple-element.9, bf16[1,768,4096]{2,1,0:T(8,128)(2,1)S(1)} %bitcast.78), kind=kOutput, calls=%fused_computation.22 | convolution fusion | flops 3223322624 | bytes 11272192 | tf_op jit(solution)/shard_map/dot_general | solution.py:40
  86.7 4.7 %all-to-all-start.4 = ((bf16[16,32,4096]{2,1,0:T(8,128)(2,1)}), bf16[16,32,4096]{2,1,0:T(8,128)(2,1)}, u32[]{:S(2)}, u32[]{:S(2)}) async-start(bf16[16,32,4096]{2,1,0:T(8,128)(2,1)} %bitcast.71), calls=%async_computation.4 | async-start | bytes 8388608 | tf_op jit(solution)/shard_map/all_to_all | solution.py:43
  91.5 0.6 copy.13
  92.1 4.4 %gather_fusion = bf16[512,4096]{1,0:T(8,128)(2,1)} fusion(bf16[128,4096]{1,0:T(8,128)(2,1)S(1)} %copy-done.2, s32[1024]{0:T(1024)S(1)} %pad_clamp_fusion), kind=kCustom, calls=%fused_computation | custom fusion | bytes 8390656 | tf_op jit(solution)/shard_map/gather | solution.py:29
  96.6 46.1 %all-to-all-done.4 = bf16[16,32,4096]{2,1,0:T(8,128)(2,1)} async-done(((bf16[16,32,4096]{2,1,0:T(8,128)(2,1)}), bf16[16,32,4096]{2,1,0:T(8,128)(2,1)}, u32[]{:S(2)}, u32[]{:S(2)}) %all-to-all-start.4) | async-done | bytes 4194336 | tf_op jit(solution)/shard_map/all_to_all | solution.py:43
  142.7 5.0 %all-to-all-start = ((bf16[16,1,32]{2,1,0:T(2,128)(2,1)}), bf16[16,1,32]{2,1,0:T(2,128)(2,1)S(1)}, u32[]{:S(2)}, u32[]{:S(2)}) async-start(bf16[16,1,32]{2,1,0:T(2,128)(2,1)} %copy.13), calls=%async_computation | async-start | bytes 16384 | tf_op jit(solution)/shard_map/all_to_all | solution.py:52
  147.7 6.5 %multiply_reduce_fusion = (bf16[16,32]{1,0:T(8,128)(2,1)}, bf16[16,32,4096]{2,1,0:T(8,128)(2,1)}) fusion(bf16[16,32,4096]{2,1,0:T(8,128)(2,1)} %all-to-all-done.4, bf16[16,32,4096]{2,1,0:T(8,128)(2,1)} %bitcast.65, pred[16,32]{1,0:T(8,128)(4,1)S(1)} %iota_compare_fusion.2), kind=kLoop, calls=%fused_computation.4 | loop fusion | flops 10485248 | bytes 12584448 | tf_op jit(solution)/shard_map/reduce_sum | solution.py:69
  154.1 6.7 %all-to-all-start.1 = ((bf16[16,32,4096]{2,1,0:T(8,128)(2,1)}), bf16[16,32,4096]{2,1,0:T(8,128)(2,1)}, u32[]{:S(2)}, u32[]{:S(2)}) async-start(bf16[16,32,4096]{2,1,0:T(8,128)(2,1)} %get-tuple-element.6), calls=%async_computation.1 | async-start | bytes 8388608 | tf_op jit(solution)/shard_map/all_to_all | solution.py:51
  161.0 47.8 %all-to-all-done.1 = bf16[16,32,4096]{2,1,0:T(8,128)(2,1)} async-done(((bf16[16,32,4096]{2,1,0:T(8,128)(2,1)}), bf16[16,32,4096]{2,1,0:T(8,128)(2,1)}, u32[]{:S(2)}, u32[]{:S(2)}) %all-to-all-start.1) | async-done | bytes 4194336 | tf_op jit(solution)/shard_map/all_to_all | solution.py:51
  208.8 3.7 %fusion = bf16[512,4096]{1,0:T(8,128)(2,1)S(1)} fusion(f32[512]{0:T(512)S(1)} %reshape.169, bf16[16,32,4096]{2,1,0:T(8,128)(2,1)} %all-to-all-done.1), kind=kLoop, calls=%fused_computation.3 | loop fusion | flops 6291456 | bytes 8390656 | tf_op jit(solution)/shard_map/convert_element_type | solution.py:56
  212.5 5.4 %convolution_convert_fusion = bf16[768,4096]{1,0:T(8,128)(2,1)} fusion(bf16[512,768]{1,0:T(8,128)(2,1)S(1)} %get-tuple-element.9, bf16[512,4096]{1,0:T(8,128)(2,1)S(1)} %fusion), kind=kOutput, calls=%fused_computation.7 | convolution fusion | flops 3224371200 | bytes 11272192 | tf_op jit(solution)/shard_map/dot_general | solution.py:14
  218.0 3.6 multiply_convert_fusion
  221.6 6.8 %multiply_convert_fusion.5 = (bf16[512,768]{1,0:T(8,128)(2,1)S(1)}, bf16[512,768]{1,0:T(8,128)(2,1)S(1)}) fusion(f32[512,768]{1,0:T(8,128)S(1)} %fusion.3, f32[512,768]{1,0:T(8,128)S(1)} %copy-done.9, bf16[512,4096]{1,0:T(8,128)(2,1)S(1)} %bitcast.66, bf16[1,768,4096]{2,1,0:T(8,128)(2,1)} %param.15), kind=kOutput, calls=%fused_computation.30 | convolution fusion | flops 3226337280 | bytes 15204352 | tf_op jit(solution)/shard_map/dot_general | solution.py:8
  228.4 5.4 %convolution_convert_fusion.1 = bf16[4096,768]{1,0:T(8,128)(2,1)} fusion(bf16[512,4096]{1,0:T(8,128)(2,1)S(1)} %bitcast.70, bf16[512,768]{1,0:T(8,128)(2,1)S(1)} %get-tuple-element.7), kind=kOutput, calls=%fused_computation.8 | convolution fusion | flops 3224371200 | bytes 11272192 | tf_op jit(solution)/shard_map/dot_general | solution.py:14
  233.8 0.3 reduce-scatter.4.cloned.1.call-start
  234.1 8.5 %convolution_convert_fusion.2 = bf16[4096,768]{1,0:T(8,128)(2,1)} fusion(bf16[512,4096]{1,0:T(8,128)(2,1)} %bitcast.69, bf16[512,768]{1,0:T(8,128)(2,1)S(1)} %get-tuple-element.8), kind=kOutput, calls=%fused_computation.9 | convolution fusion | flops 3224371200 | bytes 11272192 | tf_op jit(solution)/shard_map/dot_general | solution.py:14
  242.6 5.6 %fusion.1 = f32[512,4096]{1,0:T(8,128)S(1)} fusion(bf16[512,768]{1,0:T(8,128)(2,1)S(1)} %get-tuple-element.8, bf16[1,4096,768]{2,1,0:T(8,128)(2,1)} %param.13), kind=kOutput, calls=%fused_computation.10 | convolution fusion | flops 3221225472 | bytes 15466496 | tf_op jit(solution)/shard_map/dot_general | solution.py:8
  248.2 8.1 %add_convert_fusion = bf16[512,4096]{1,0:T(8,128)(2,1)} fusion(f32[512,4096]{1,0:T(8,128)S(1)} %fusion.1, bf16[512,768]{1,0:T(8,128)(2,1)S(1)} %get-tuple-element.7, bf16[1,4096,768]{2,1,0:T(8,128)(2,1)} %param.14), kind=kOutput, calls=%fused_computation.5 | convolution fusion | flops 3225419776 | bytes 19660800 | tf_op jit(solution)/shard_map/dot_general | solution.py:8
  256.4 9.6 %all-to-all-start.3 = ((bf16[16,32,4096]{2,1,0:T(8,128)(2,1)}), bf16[16,32,4096]{2,1,0:T(8,128)(2,1)}, u32[]{:S(2)}, u32[]{:S(2)}) async-start(bf16[16,32,4096]{2,1,0:T(8,128)(2,1)} %bitcast.72), calls=%async_computation.3 | async-start | bytes 8388608 | tf_op jit(solution)/shard_map/all_to_all | solution.py:68
  266.1 45.9 %all-to-all-done.3 = bf16[16,32,4096]{2,1,0:T(8,128)(2,1)} async-done(((bf16[16,32,4096]{2,1,0:T(8,128)(2,1)}), bf16[16,32,4096]{2,1,0:T(8,128)(2,1)}, u32[]{:S(2)}, u32[]{:S(2)}) %all-to-all-start.3) | async-done | bytes 4194336 | tf_op jit(solution)/shard_map/all_to_all | solution.py:68
  312.0 4.0 %convolution_convert_fusion.3 = bf16[128,4096]{1,0:T(8,128)(2,1)} fusion(bf16[512,4096]{1,0:T(8,128)(2,1)} %bitcast.12, s32[512]{0:T(512)S(1)} %eq.15, pred[512]{0:T(512)(128)(4,1)S(1)} %lt.46), kind=kOutput, calls=%fused_computation.23 | convolution fusion | flops 537526272 | bytes 5245440 | tf_op jit(solution)/shard_map/dot_general | solution.py:93
  316.0 2.2 fusion.21
  318.2 2.1 fusion.20
  320.3 36.8 %reduce-scatter.4.cloned.1.call-done = bf16[512,768]{1,0:T(8,128)(2,1)} async-done(((bf16[4096,768]{1,0:T(8,128)(2,1)}), bf16[512,768]{1,0:T(8,128)(2,1)}) %reduce-scatter.4.cloned.1.call-update) | async-done | bytes 786448 | tf_op jit(solution)/shard_map/reduce_scatter | solution.py:76
  357.1 2.1 fusion.19
  (46 shorter events, 0.6 us)
Async XLA Ops:
  7.2 1.6 copy-start
  13.1 60.4 %copy-start.8 = (bf16[1,4096,768]{2,1,0:T(8,128)(2,1)S(1)}, bf16[1,4096,768]{2,1,0:T(8,128)(2,1)}, u32[]{:S(2)}) copy-start(bf16[1,4096,768]{2,1,0:T(8,128)(2,1)} %param.13) | copy-start | bytes 18874372
  15.8 61.2 %slice-start.2 = ((s8[6291456]{0:T(1024)(128)(4,1)}), s8[4194304]{0:T(1024)(128)(4,1)S(1)}, s32[]{:S(2)}) async-start(s8[6291456]{0:T(1024)(128)(4,1)} %bitcast.79), calls=%async_computation.13 | async-start | bytes 8388608
  15.8 65.8 %slice-start = ((s8[6291456]{0:T(1024)(128)(4,1)}), s8[4194304]{0:T(1024)(128)(4,1)S(1)}, s32[]{:S(2)}) async-start(s8[6291456]{0:T(1024)(128)(4,1)} %bitcast.77), calls=%async_computation.11 | async-start | bytes 8388608
  73.6 3.5 copy-start.3
  73.6 3.5 slice-start.3
  73.6 8.1 %slice-start.1 = ((s8[6291456]{0:T(1024)(128)(4,1)}), s8[2097152]{0:T(1024)(128)(4,1)S(1)}, s32[]{:S(2)}) async-start(s8[6291456]{0:T(1024)(128)(4,1)} %bitcast.77), calls=%async_computation.12 | async-start | bytes 4194304
  86.7 4.7 %copy-start.6 = (bf16[1,16,32]{2,1,0:T(8,128)(2,1)S(1)}, bf16[1,16,32]{2,1,0:T(8,128)(2,1)}, u32[]{:S(2)}) copy-start(bf16[1,16,32]{2,1,0:T(8,128)(2,1)} %param.12) | copy-start | bytes 3076
  86.7 4.7 %copy-start.7 = (s32[1,16]{1,0:T(1,128)S(1)}, s32[1,16]{1,0:T(1,128)}, u32[]{:S(2)}) copy-start(s32[1,16]{1,0:T(1,128)} %param.11) | copy-start | bytes 196
  86.7 5.4 %copy-start.2 = (bf16[128,4096]{1,0:T(8,128)(2,1)S(1)}, bf16[128,4096]{1,0:T(8,128)(2,1)}, u32[]{:S(2)}) copy-start(bf16[128,4096]{1,0:T(8,128)(2,1)} %param.9) | copy-start | bytes 3145732
  86.7 56.0 %all-to-all-start.4 = ((bf16[16,32,4096]{2,1,0:T(8,128)(2,1)}), bf16[16,32,4096]{2,1,0:T(8,128)(2,1)}, u32[]{:S(2)}, u32[]{:S(2)}) async-start(bf16[16,32,4096]{2,1,0:T(8,128)(2,1)} %bitcast.71), calls=%async_computation.4 | async-start | bytes 8388608 | tf_op jit(solution)/shard_map/all_to_all | solution.py:43
  142.7 11.4 %all-to-all-start = ((bf16[16,1,32]{2,1,0:T(2,128)(2,1)}), bf16[16,1,32]{2,1,0:T(2,128)(2,1)S(1)}, u32[]{:S(2)}, u32[]{:S(2)}) async-start(bf16[16,1,32]{2,1,0:T(2,128)(2,1)} %copy.13), calls=%async_computation | async-start | bytes 16384 | tf_op jit(solution)/shard_map/all_to_all | solution.py:52
  154.1 54.6 %all-to-all-start.1 = ((bf16[16,32,4096]{2,1,0:T(8,128)(2,1)}), bf16[16,32,4096]{2,1,0:T(8,128)(2,1)}, u32[]{:S(2)}, u32[]{:S(2)}) async-start(bf16[16,32,4096]{2,1,0:T(8,128)(2,1)} %get-tuple-element.6), calls=%async_computation.1 | async-start | bytes 8388608 | tf_op jit(solution)/shard_map/all_to_all | solution.py:51
  160.9 155.1 %reduce-scatter.8.cloned.1.call-start = ((), (), s32[]{:S(2)}) async-start(), calls=%async_computation.10 | async-start | bytes 7077888 | tf_op jit(solution)/shard_map/reduce_scatter | solution.py:82
  217.9 100.3 %reduce-scatter.6.cloned.1.call-start = ((), (), s32[]{:S(2)}) async-start(), calls=%async_computation.9 | async-start | bytes 7077888 | tf_op jit(solution)/shard_map/reduce_scatter | solution.py:79
  218.0 3.6 copy-start.9
  221.6 6.8 %copy-start.4 = (bf16[16,32,4096]{2,1,0:T(8,128)(2,1)S(1)}, bf16[16,32,4096]{2,1,0:T(8,128)(2,1)}, u32[]{:S(2)}) copy-start(bf16[16,32,4096]{2,1,0:T(8,128)(2,1)} %copy-done.3) | copy-start | bytes 12582916
  233.8 123.3 %reduce-scatter.4.cloned.1.call-start = ((), (), s32[]{:S(2)}) async-start(), calls=%async_computation.8 | async-start | bytes 7077888 | tf_op jit(solution)/shard_map/reduce_scatter | solution.py:76
  256.4 9.7 %copy-start.5 = (s32[1,16,32]{2,1,0:T(8,128)S(1)}, s32[1,16,32]{2,1,0:T(8,128)}, u32[]{:S(2)}) copy-start(s32[1,16,32]{2,1,0:T(8,128)} %param.10) | copy-start | bytes 6148
  256.4 55.7 %all-to-all-start.3 = ((bf16[16,32,4096]{2,1,0:T(8,128)(2,1)}), bf16[16,32,4096]{2,1,0:T(8,128)(2,1)}, u32[]{:S(2)}, u32[]{:S(2)}) async-start(bf16[16,32,4096]{2,1,0:T(8,128)(2,1)} %bitcast.72), calls=%async_computation.3 | async-start | bytes 8388608 | tf_op jit(solution)/shard_map/all_to_all | solution.py:68
  312.0 47.2 %copy-start.1 = (bf16[128,4096]{1,0:T(8,128)(2,1)S(1)}, bf16[128,4096]{1,0:T(8,128)(2,1)}, u32[]{:S(2)}) copy-start(bf16[128,4096]{1,0:T(8,128)(2,1)} %param.8) | copy-start | bytes 3145732
Sparse Core Ops, SparseCore 0:
  218.0 49.2 reduce-scatter.7
  269.8 42.1 reduce-scatter.5
  314.3 42.7 reduce-scatter.3
where the time goes:
time: 366 us
  waiting for transfers between devices  177 us (48%)
  blocking collectives  57.7 us (16%)
  matrix products  56.8 us (16%)
  starting transfers between devices  26.3 us (7%)
  other arithmetic  24.5 us (7%)
  between operations  14 us (4%)
  local copies, waits for them, and re-layouts  9.78 us (3%)
    all_to_all x1, blocking collectives, shards(): lax.all_to_all(send_x, 'expert', split_axis=0, concat_axis=0, tiled=True)  57.7 us
    all_to_all x1, waiting for transfers between devices, shards(): lax.all_to_all(send_dy, 'expert', split_axis=0, concat_axis=0, tiled=True)  47.8 us
    all_to_all x1, waiting for transfers between devices, shards(): lax.all_to_all(expert_out.reshape(experts, capacity, width), 'expert', sp...  46.1 us
    all_to_all x1, waiting for transfers between devices, shards(): lax.all_to_all(input_grad, 'expert', split_axis=0, concat_axis=0, tiled=T...  45.9 us
    reduce_scatter x1, waiting for transfers between devices, shards(): lax.psum_scatter(part_gate.astype(jnp.bfloat16), 'dp', scatter_dimension=...  36.8 us
    dot_general x3, matrix products, contract_last(): lax.dot_general(left, right, (((1,), (1,)), ((), ())), preferred_element_...  20.5 us
    dot_general x3, matrix products, contract_first(): lax.dot_general(left, right, (((0,), (0,)), ((), ())), preferred_element_...  19.2 us
    all_to_all x1, starting transfers between devices, shards(): lax.all_to_all(input_grad, 'expert', split_axis=0, concat_axis=0, tiled=T...  9.6 us
  transfers between devices with their start and end apart: 7, of which 4 were waited for; matrix products, arithmetic and copies ran while one was open for 16% of the time, Pallas kernels for 0%

commit v1 on v0

v1 whole, which is shorter than its diff:
```python
import jax
import jax.numpy as jnp
from jax import lax
from jax.experimental import pallas as pl
from jax.experimental.pallas import tpu as pltpu
from jax.sharding import PartitionSpec as P

MESH = pl.DeviceIdType.MESH
BF = jnp.bfloat16
F32 = jnp.float32
D = 4096
FF = 768
TOK = 128
EXP = 16
CAP = 32
ROWS = EXP * CAP
NCH = 4
W = D // NCH
PIECE = W // 8
HALF = W // 2
UNITS = 3 * NCH
SEND = 3
NWGU = 2
NWD = 2


def feature(chunk, block):
    return (2 * (block % 4) + block // 4) * (D // 8) + chunk * PIECE


def contract(left, right, dims):
    return lax.dot_general(left, right, (dims, ((), ())), preferred_element_type=F32)


def body(
    pick_ref, pick_prob_ref, place_ref, prob_ref, tok_ref, dy_ref, wg_hbm, wu_hbm, wd_hbm,
    tg_ref, route_ref, gg_ref, gu_ref, gd_ref,
    send, got_x, got_y, wgu, wdn, acc, hgrad, hidden, grads, got_back, rbuf, got_r,
    lhs_t, own, mate_out, mate_in, total, far, near, relay,
    disp_s, disp_r, disp_l, back_s, back_r, back_l, rs_s, rs_r, rs_l, wgu_sem, wdn_sem,
    mate_s, mate_r, ring_s, ring_r,
):
    dp = lax.axis_index("dp")
    me = lax.axis_index("expert")
    y, core = dp // 2, lax.rem(dp, 2)
    x, z = me // 4, lax.rem(me, 4)

    def peer(k):
        return lax.rem(x + k // 4, 4) * 4 + lax.rem(z + lax.rem(k, 4), 4)

    def on_expert(e):
        return {"dp": dp, "expert": e}

    mate = {"dp": y * 2 + 1 - core, "expert": me}
    y_dn, y_up, y_far = lax.rem(y + 3, 4), lax.rem(y + 1, 4), lax.rem(y + 2, 4)
    side = ({"dp": y_dn * 2 + core, "expert": me}, {"dp": y_up * 2 + core, "expert": me})

    def each_peer(fn):
        def step(i, carry):
            fn(1 + i)
            return carry
        lax.fori_loop(0, EXP - 1, step, 0)

    def load_gu(chunk, slot):
        for b in range(8):
            rows = pl.ds(feature(chunk, b), PIECE)
            here = pl.ds(b * PIECE, PIECE)
            pltpu.make_async_copy(wg_hbm.at[rows, :], wgu.at[slot, here, pl.ds(0, FF)], wgu_sem.at[slot]).start()
            pltpu.make_async_copy(wu_hbm.at[rows, :], wgu.at[slot, here, pl.ds(FF, FF)], wgu_sem.at[slot]).start()

    def wait_gu(slot):
        pltpu.make_async_copy(wgu.at[slot], wgu.at[slot], wgu_sem.at[slot]).wait()

    def load_dn(chunk, slot):
        for b in range(8):
            pltpu.make_async_copy(
                wd_hbm.at[:, pl.ds(feature(chunk, b), PIECE)],
                wdn.at[slot, :, pl.ds(b * PIECE, PIECE)], wdn_sem.at[slot]).start()

    def wait_dn(slot):
        pltpu.make_async_copy(wdn.at[slot], wdn.at[slot], wdn_sem.at[slot]).wait()

    for c in range(NWGU):
        load_gu(c, c)
    for c in range(NWD):
        load_dn(c, c)

    barrier = pltpu.get_barrier_semaphore()

    def greet(k):
        pl.semaphore_signal(barrier, inc=1, device_id=on_expert(peer(k)), device_id_type=MESH)

    each_peer(greet)
    for there in (mate, side[0], side[1]):
        pl.semaphore_signal(barrier, inc=1, device_id=there, device_id_type=MESH)

    def gather(t):
        source, select = (tok_ref, pick_ref) if t < NCH else (dy_ref, pick_prob_ref)
        c = t % NCH
        for h in range(2):
            rhs = jnp.concatenate(
                [source[:, feature(c, 4 * h + b):feature(c, 4 * h + b) + PIECE] for b in range(4)], axis=1)
            rows = contract(select[...], rhs, ((1,), (0,))).astype(BF)
            send[t % SEND, :, :, h * HALF:(h + 1) * HALF] = rows.reshape(EXP, CAP, HALF)

    def landing(t):
        return (got_x if t < NCH else got_y).at[t % NCH]

    def disp_copy(t, k):
        return pltpu.make_async_remote_copy(
            src_ref=send.at[t % SEND, peer(k)], dst_ref=landing(t).at[me],
            send_sem=disp_s.at[t, k], recv_sem=disp_r.at[t, k],
            device_id=on_expert(peer(k)), device_id_type=MESH)

    def disp_local(t):
        return pltpu.make_async_copy(send.at[t % SEND, me], landing(t).at[me], disp_l.at[t])

    def disp_start(t):
        each_peer(lambda k: disp_copy(t, k).start())
        disp_local(t).start()

    def disp_sent(t):
        each_peer(lambda k: disp_copy(t, k).wait_send())

    def disp_wait(t):
        disp_local(t).wait()
        each_peer(lambda k: disp_copy(t, k).wait_recv())

    def unit(u):
        if u < NCH:
            return got_y.at[u], hidden, 0
        v = u - NCH
        return got_x.at[v // 2], grads, (v % 2) * FF

    def product(u, core_half, write):
        rows, right, col = unit(u)
        start = pl.multiple_of(core_half * HALF, HALF)
        lhs_t[...] = rows[:, :, pl.ds(start, HALF)].reshape(ROWS, HALF).T
        for n in range(3):
            cols = slice(n * 256, (n + 1) * 256)
            write(cols, contract(lhs_t[...], right[:, col + n * 256:col + (n + 1) * 256], ((1,), (0,))))

    def mate_copy(u):
        return pltpu.make_async_remote_copy(
            src_ref=mate_out.at[u % 2], dst_ref=mate_in.at[u], send_sem=mate_s.at[u], recv_sem=mate_r.at[u],
            device_id=mate, device_id_type=MESH)

    def ring_copy(u, i):
        kind, way = i // 2, i % 2
        lower, upper = pl.ds(0, PIECE // 2), pl.ds(PIECE // 2, PIECE // 2)
        owner = (y_far, (y_dn, y_up)[way], (y_dn, y_up)[way])[kind]
        part = (lower, upper)[(way, 1 - way, way)[kind]]
        return pltpu.make_async_remote_copy(
            src_ref=total.at[u % 3, owner, part, :], dst_ref=(far, near, relay)[kind].at[u, way],
            send_sem=ring_s.at[u, i], recv_sem=ring_r.at[u, i],
            device_id=side[way], device_id_type=MESH)

    def stage0(u):
        if u >= 2:
            mate_copy(u - 2).wait_send()

        def to_mate(cols, value):
            mate_out[u % 2, :, cols] = value.astype(BF)

        def to_own(cols, value):
            own[:, cols] = value

        product(u, 1 - core, to_mate)
        mate_copy(u).start()
        product(u, core, to_own)

    def stage1(u):
        if u >= 3:
            for i in range(6):
                ring_copy(u - 3, i).wait_send()
        mate_copy(u).wait_recv()
        for q in range(4):
            rows = slice(q * PIECE, (q + 1) * PIECE)
            total[u % 3, q] = (own[rows, :] + mate_in[u, rows, :].astype(F32)).astype(BF)
        for i in range(4):
            ring_copy(u, i).start()

    def stage2(u):
        half = PIECE // 2
        for way, owner in ((0, y_dn), (1, y_up)):
            ring_copy(u, way).wait_recv()
            rows = slice(way * half, (way + 1) * half)
            total[u % 3, owner, rows, :] = (
                total[u % 3, owner, rows, :].astype(F32) + far[u, way].astype(F32)).astype(BF)
            ring_copy(u, 4 + way).start()

    def stage3(u):
        half = PIECE // 2
        for i in range(2, 6):
            ring_copy(u, i).wait_recv()
        halves = []
        for h in range(2):
            rows = slice(h * half, (h + 1) * half)
            halves.append((total[u % 3, y, rows, :].astype(F32) + near[u, 1 - h].astype(F32)
                           + relay[u, h].astype(F32)) * 0.125)
        whole = jnp.concatenate(halves, axis=0)
        if u < NCH:
            gd_ref[:, u * PIECE:(u + 1) * PIECE] = whole.T.astype(BF)
        else:
            v = u - NCH
            (gg_ref, gu_ref)[v % 2][(v // 2) * PIECE:(v // 2 + 1) * PIECE, :] = whole.astype(BF)

    def tick(t):
        if 0 <= t - 1 < UNITS:
            stage1(t - 1)
        if t < UNITS:
            stage0(t)
        if 0 <= t - 2 < UNITS:
            stage2(t - 2)
        if 0 <= t - 3 < UNITS:
            stage3(t - 3)

    def forward(c):
        disp_wait(c)
        wait_gu(c % NWGU)

        def step(n, carry):
            cols = pl.ds(pl.multiple_of(n * 256, 256), 256)
            part = contract(got_x[c].reshape(ROWS, W), wgu[c % NWGU, :, cols], ((1,), (0,)))
            if c == 0:
                acc[:, cols] = part
            else:
                acc[:, cols] += part
            return carry

        lax.fori_loop(0, 2 * FF // 256, step, 0)
        load_gu((c + NWGU) % NCH, c % NWGU)

    def activate():
        def step(i, carry):
            rows = pl.ds(pl.multiple_of(i * CAP, CAP), CAP)
            gate, up = acc[rows, :FF], acc[rows, FF:]
            sig = jax.nn.sigmoid(gate)
            act = gate * sig
            hidden[rows, :] = (act * up).astype(BF)
            acc[rows, :FF] = up * sig * (1.0 + gate * (1.0 - sig))
            acc[rows, FF:] = act
            return carry

        lax.fori_loop(0, EXP, step, 0)

    def backward(c):
        disp_wait(NCH + c)
        wait_dn(c % NWD)
        rows = got_y[c].reshape(ROWS, W)
        for n in range(3):
            cols = slice(n * 256, (n + 1) * 256)
            part = contract(rows, wdn[c % NWD, cols, :], ((1,), (1,)))
            if c == 0:
                hgrad[:, cols] = part
            else:
                hgrad[:, cols] += part
        if c + NWD < NCH:
            load_dn(c + NWD, c % NWD)

    def route_copy(k):
        return pltpu.make_async_remote_copy(
            src_ref=rbuf.at[peer(k)], dst_ref=got_r.at[me], send_sem=rs_s.at[k], recv_sem=rs_r.at[k],
            device_id=on_expert(peer(k)), device_id_type=MESH)

    def route_local():
        return pltpu.make_async_copy(rbuf.at[me], got_r.at[me], rs_l.at[0])

    def differentiate():
        def step(i, carry):
            rows = pl.ds(pl.multiple_of(i * CAP, CAP), CAP)
            grad = hgrad[rows, :]
            grads[rows, :FF] = (grad * acc[rows, :FF]).astype(BF)
            grads[rows, FF:] = (grad * acc[rows, FF:]).astype(BF)
            dot = jnp.sum(grad * hidden[rows, :].astype(F32), axis=1, keepdims=True)
            rbuf[i] = jnp.broadcast_to(dot, (CAP, 128))
            return carry

        lax.fori_loop(0, EXP, step, 0)

    def back_copy(c, k):
        return pltpu.make_async_remote_copy(
            src_ref=got_y.at[c, peer(k)], dst_ref=got_back.at[c, me], send_sem=back_s.at[c, k],
            recv_sem=back_r.at[c, k], device_id=on_expert(peer(k)), device_id_type=MESH)

    def back_local(c):
        return pltpu.make_async_copy(got_y.at[c, me], got_back.at[c, me], back_l.at[c])

    def give_back(c):
        wait_gu(c % NWGU)
        for n in range(W // 256):
            cols = slice(n * 256, (n + 1) * 256)
            part = contract(grads[...], wgu[c % NWGU, cols, :], ((1,), (1,)))
            got_y[c, :, :, cols] = part.astype(BF).reshape(EXP, CAP, 256)
        each_peer(lambda k: back_copy(c, k).start())
        back_local(c).start()
        if c + NWGU < NCH:
            load_gu(c + NWGU, c % NWGU)

    def combine(c):
        back_local(c).wait()
        each_peer(lambda k: back_copy(c, k).wait_recv())
        for h in range(2):
            rows = got_back[c, :, :, h * HALF:(h + 1) * HALF].reshape(ROWS, HALF)
            part = contract(place_ref[...], rows, ((1,), (0,))).astype(BF)
            for b in range(4):
                f = feature(c, 4 * h + b)
                tg_ref[:, f:f + PIECE] = part[:, b * PIECE:(b + 1) * PIECE]

    gather(0)
    gather(1)
    pl.semaphore_wait(barrier, EXP - 1 + 3)
    disp_start(0)
    disp_start(1)
    gather(2)
    disp_start(2)
    for t in range(2 * NCH):
        if t < NCH:
            forward(t)
        if t == NCH - 1:
            activate()
        if t >= NCH:
            backward(t - NCH)
        if t + SEND < 2 * NCH:
            disp_sent(t)
            gather(t + SEND)
            disp_start(t + SEND)
        if t >= NCH:
            tick(t - NCH)
    differentiate()
    each_peer(lambda k: route_copy(k).start())
    route_local().start()
    last = UNITS + 3
    for t in range(NCH, last):
        tick(t)
        r = t - NCH
        if r < NCH:
            give_back(r)
        if r >= 3 and r % 2 == 1 and (r - 3) // 2 < NCH:
            combine((r - 3) // 2)
    route_local().wait()
    each_peer(lambda k: route_copy(k).wait_recv())
    lane = lax.broadcasted_iota(jnp.int32, (EXP, CAP, 128), 2)
    slot = lax.broadcasted_iota(jnp.int32, (EXP, CAP, 128), 1)
    dots = jnp.sum(jnp.where(lane == slot, got_r[...], 0.0), axis=1)[:, :CAP]
    prob = prob_ref[...].astype(F32)
    live = prob > 0.0
    route_ref[...] = jnp.where(live, dots / jnp.where(live, prob, 1.0), 0.0).astype(BF)
    for t in range(2 * NCH - SEND, 2 * NCH):
        disp_sent(t)
    for c in range(NCH):
        each_peer(lambda k: back_copy(c, k).wait_send())
    each_peer(lambda k: route_copy(k).wait_send())
    for u in range(UNITS - 2, UNITS):
        mate_copy(u).wait_send()
    for u in range(UNITS - 3, UNITS):
        for i in range(6):
            ring_copy(u, i).wait_send()


def shards(tokens, out_grad, group_token, group_count, group_prob, w_gate, w_up, w_down):
    index, prob = group_token[0], group_prob[0]
    live = lax.broadcasted_iota(jnp.int32, (EXP, CAP), 1) < group_count[0][:, None]
    index = jnp.where(live, index, -1).reshape(ROWS)
    prob = jnp.where(live, prob, jnp.zeros((), BF))
    hit = index[:, None] == lax.broadcasted_iota(jnp.int32, (ROWS, TOK), 1)
    pick = hit.astype(BF)
    pick_prob = jnp.where(hit, prob.reshape(ROWS)[:, None], jnp.zeros((), BF))
    place = (index[None, :] == lax.broadcasted_iota(jnp.int32, (TOK, ROWS), 0)).astype(BF)
    vmem = pl.BlockSpec(memory_space=pltpu.VMEM)
    hbm = pl.BlockSpec(memory_space=pl.ANY)
    dma = pltpu.SemaphoreType.DMA
    token_grad, route_grad, grad_gate, grad_up, grad_down = pl.pallas_call(
        body,
        out_shape=(
            jax.ShapeDtypeStruct((TOK, D), BF),
            jax.ShapeDtypeStruct((EXP, CAP), BF),
            jax.ShapeDtypeStruct((D // 8, FF), BF),
            jax.ShapeDtypeStruct((D // 8, FF), BF),
            jax.ShapeDtypeStruct((FF, D // 8), BF),
        ),
        in_specs=[vmem] * 6 + [hbm] * 3,
        out_specs=[vmem] * 5,
        scratch_shapes=[
            pltpu.VMEM((SEND, EXP, CAP, W), BF),
            pltpu.VMEM((NCH, EXP, CAP, W), BF),
            pltpu.VMEM((NCH, EXP, CAP, W), BF),
            pltpu.VMEM((NWGU, W, 2 * FF), BF),
            pltpu.VMEM((NWD, FF, W), BF),
            pltpu.VMEM((ROWS, 2 * FF), F32),
            pltpu.VMEM((ROWS, FF), F32),
            pltpu.VMEM((ROWS, FF), BF),
            pltpu.VMEM((ROWS, 2 * FF), BF),
            pltpu.VMEM((NCH, EXP, CAP, W), BF),
            pltpu.VMEM((EXP, CAP, 128), F32),
            pltpu.VMEM((EXP, CAP, 128), F32),
            pltpu.VMEM((HALF, ROWS), BF),
            pltpu.VMEM((HALF, FF), F32),
            pltpu.VMEM((2, HALF, FF), BF),
            pltpu.VMEM((UNITS, HALF, FF), BF),
            pltpu.VMEM((3, 4, PIECE, FF), BF),
            pltpu.VMEM((UNITS, 2, PIECE // 2, FF), BF),
            pltpu.VMEM((UNITS, 2, PIECE // 2, FF), BF),
            pltpu.VMEM((UNITS, 2, PIECE // 2, FF), BF),
            dma((2 * NCH, EXP)), dma((2 * NCH, EXP)), dma((2 * NCH,)),
            dma((NCH, EXP)), dma((NCH, EXP)), dma((NCH,)),
            dma((EXP,)), dma((EXP,)), dma((1,)),
            dma((NWGU,)), dma((NWD,)),
            dma((UNITS,)), dma((UNITS,)), dma((UNITS, 6)), dma((UNITS, 6)),
        ],
        compiler_params=pltpu.CompilerParams(
            collective_id=0, has_side_effects=True, vmem_limit_bytes=64 << 20),
        cost_estimate=pl.CostEstimate(flops=8 * 2 * ROWS * D * FF, bytes_accessed=40 << 20, transcendentals=ROWS * FF),
    )(pick, pick_prob, place, prob, tokens, out_grad, w_gate[0], w_up[0], w_down[0])
    return token_grad, route_grad[None], grad_gate[None], grad_up[None], grad_down[None]


def solution(mesh):
    slots = P(("dp", "expert"), None, None)
    rows = P(("dp", "expert"), None)
    experts = P("expert", None, None)
    return jax.shard_map(
        shards, mesh=mesh,
        in_specs=(rows, rows, slots, rows, slots, experts, experts, experts),
        out_specs=(rows, slots, P("expert", "dp", None), P("expert", "dp", None), P("expert", None, "dp")),
        check_vma=False)
```

time: 366 us -> 196 us (0.54)
  Pallas kernels: 0 us -> 179 us
  waiting for transfers between devices: 177 us -> 0 us
  blocking collectives: 57.7 us -> 0 us
  matrix products: 56.8 us -> 0 us
  starting transfers between devices: 26.3 us -> 0 us
  other arithmetic: 24.5 us -> 4.42 us
  between operations: 14 us -> 0.65 us
    pallas_call x0 -> x1, Pallas kernels: none -> 179 us  [shards(): pl.pallas_call(body, out_shape=(jax.ShapeDtypeStruct((TOK, D), BF), jax.S...]
    all_to_all x4 -> x0, waiting for transfers between devices: 140 us -> none  [the longest x1 47.8 us: shards(): lax.all_to_all(send_dy, 'expert', split_axis=0, concat_axis=0, tiled=True)]
    all_to_all x1 -> x0, blocking collectives: 57.7 us -> none  [shards(): lax.all_to_all(send_x, 'expert', split_axis=0, concat_axis=0, tiled=True)]
    dot_general x10 -> x0, matrix products: 56.8 us -> none  [the longest x3 20.5 us: contract_last(): lax.dot_general(left, right, (((1,), (1,)), ((), ())), preferred_element_...]
    reduce_scatter x3 -> x0, waiting for transfers between devices: 36.8 us -> none  [the longest x1 36.8 us: shards(): lax.psum_scatter(part_gate.astype(jnp.bfloat16), 'dp', scatter_dimension=...]
    all_to_all x4 -> x0, starting transfers between devices: 26 us -> none  [the longest x1 9.6 us: shards(): lax.all_to_all(input_grad, 'expert', split_axis=0, concat_axis=0, tiled=T...]
    unnamed x28 -> x5, local copies, waits for them, and re-layouts: 0.07 us -> 9.74 us
    gather x2 -> x0, local copies, waits for them, and re-layouts: 8.78 us -> none  [the longest x1 4.43 us: shards(): send_dy = jnp.where(live_slot[..., None], out_grad[tok_index], zero_half)]
  transfers between devices with their start and end apart: 7 -> 0, of which waited for: 4 -> 0; matrix products, arithmetic and copies ran while one was open for 16% -> 0% of each run, Pallas kernels for 0% -> 0%
where the time goes in v1:
time: 196 us; the launch traced here: 195 us
  Pallas kernels  179 us (91%)
  local copies, waits for them, and re-layouts  11.4 us (6%)
  other arithmetic  4.42 us (2%)
    pallas_call x1, Pallas kernels, shards(): pl.pallas_call(body, out_shape=(jax.ShapeDtypeStruct((TOK, D), BF), jax.S...  179 us
    unnamed x5, local copies, waits for them, and re-layouts  9.74 us

profile of v1, /device:TPU:1, one launch (start us, length us, event | category | flops | bytes accessed | tf_op | source)
XLA Modules:
  0.0 195.4 jit_solution(12152729934876263586)
XLA Ops:
  0.6 0.8 squeeze.18
  1.4 0.8 squeeze.17
  2.2 0.7 iota_compare_fusion.2
  2.9 0.1 lt.27
  3.0 1.4 bitcast_select_fusion.prob_ref
  4.4 0.9 fusion.pick_prob_ref
  5.2 0.7 fusion.2.place_ref
  5.9 0.8 fusion.1.pick_ref
  6.7 178.9 %shard_map.119 = (bf16[128,4096]{1,0:T(8,128)(2,1)}, bf16[16,32]{1,0:T(8,128)(2,1)}, bf16[512,768]{1,0:T(8,128)(2,1)}, bf16[512,768]{1,0:T(8,128)(2,1)}, bf16[768,512]{1,0:T(8,128)(2,1)}) custom-call(bf16[512,128]{1,0:T(8,128)(2,1)} %fusion.1.pick_ref, bf16[512,128]{1,0:T(8,128)(2,1)} %fusion.pick_prob_ref, bf16[128,512]{1,0:T(8,128)(2,1)} %fusion.2.place_ref, ...), custom_call_target="tpu_custom_call" | custom-call | flops 25769803776 | bytes 41943040 | tf_op jit(solution)/shard_map/pallas_call | solution.py:373
  185.6 2.3 %copy.18 = bf16[128,4096]{1,0:T(8,128)(2,1)} copy(bf16[128,4096]{1,0:T(8,128)(2,1)} %get-tuple-element.20) | data formatting | bytes 2097152
  187.9 1.3 copy.19
  189.2 2.1 %copy.20 = bf16[1,512,768]{2,1,0:T(8,128)(2,1)} copy(bf16[1,512,768]{2,1,0:T(8,128)(2,1)} %bitcast.12) | data formatting | bytes 1572864
  191.2 2.1 %copy.21 = bf16[1,512,768]{2,1,0:T(8,128)(2,1)} copy(bf16[1,512,768]{2,1,0:T(8,128)(2,1)} %bitcast.11) | data formatting | bytes 1572864
  193.3 2.1 %copy.22 = bf16[1,768,512]{2,1,0:T(8,128)(2,1)} copy(bf16[1,768,512]{2,1,0:T(8,128)(2,1)} %bitcast.10) | data formatting | bytes 1572864
  (2 shorter events, 0.0 us)

commit v2 on v1

--- a/solution.py
+++ b/solution.py
@@ -19,7 +19,11 @@
 PIECE = W // 8
 HALF = W // 2
 UNITS = 3 * NCH
-SEND = 3
+SEND = 4
+LINE = 4
+STEPS = 4 * NCH
+SLOTS = 8
+OPEN, PASS, PICK = 7, 5, 2
 NWGU = 2
 NWD = 2
 
@@ -33,11 +37,11 @@
 
 
 def body(
-    pick_ref, pick_prob_ref, place_ref, prob_ref, tok_ref, dy_ref, wg_hbm, wu_hbm, wd_hbm,
-    tg_ref, route_ref, gg_ref, gu_ref, gd_ref,
-    send, got_x, got_y, wgu, wdn, acc, hgrad, hidden, grads, got_back, rbuf, got_r,
+    index_ref, count_ref, prob_ref, tok_hbm, dy_hbm, wg_hbm, wu_hbm, wd_hbm,
+    tg_hbm, route_ref, gg_hbm, gu_hbm, gd_hbm,
+    pick_ref, place_ref, tg_ref, gg_ref, gu_ref, gd_ref, out_sem, weigh, line, send, got_x, got_y, wgu, wdn, acc, hgrad, hidden, grads, got_back, rbuf, got_r,
     lhs_t, own, mate_out, mate_in, total, far, near, relay,
-    disp_s, disp_r, disp_l, back_s, back_r, back_l, rs_s, rs_r, rs_l, wgu_sem, wdn_sem,
+    info_s, info_r, fill_sem, line_s, line_r, free, disp_s, disp_r, disp_l, back_s, back_r, back_l, rs_s, rs_r, rs_l, wgu_sem, wdn_sem,
     mate_s, mate_r, ring_s, ring_r,
 ):
     dp = lax.axis_index("dp")
@@ -80,11 +84,6 @@
     def wait_dn(slot):
         pltpu.make_async_copy(wdn.at[slot], wdn.at[slot], wdn_sem.at[slot]).wait()
 
-    for c in range(NWGU):
-        load_gu(c, c)
-    for c in range(NWD):
-        load_dn(c, c)
-
     barrier = pltpu.get_barrier_semaphore()
 
     def greet(k):
@@ -94,37 +93,124 @@
     for there in (mate, side[0], side[1]):
         pl.semaphore_signal(barrier, inc=1, device_id=there, device_id_type=MESH)
 
-    def gather(t):
-        source, select = (tok_ref, pick_ref) if t < NCH else (dy_ref, pick_prob_ref)
-        c = t % NCH
-        for h in range(2):
-            rhs = jnp.concatenate(
-                [source[:, feature(c, 4 * h + b):feature(c, 4 * h + b) + PIECE] for b in range(4)], axis=1)
-            rows = contract(select[...], rhs, ((1,), (0,))).astype(BF)
-            send[t % SEND, :, :, h * HALF:(h + 1) * HALF] = rows.reshape(EXP, CAP, HALF)
+    def ends(t):
+        return (x, lambda q: q * 4 + z) if t % 2 == 0 else (z, lambda q: x * 4 + q)
+
+    def fill(t):
+        source = tok_hbm if t < 2 * NCH else dy_hbm
+        place = ends(t)[0]
+        for b in range(4):
+            pltpu.make_async_copy(
+                source.at[:, pl.ds(feature((t // 2) % NCH, 4 * (t % 2) + b), PIECE)],
+                line.at[t % SLOTS, place, :, pl.ds(b * PIECE, PIECE)], fill_sem.at[t]).start()
+
+    def line_copy(t, i):
+        place, expert_at = ends(t)
+        up, dn = lax.rem(place + 1, LINE), lax.rem(place + 3, LINE)
+        owner = (place, place, dn, up)[i]
+        rows = (pl.ds(0, TOK), pl.ds(0, TOK), pl.ds(0, TOK // 2), pl.ds(TOK // 2, TOK // 2))[i]
+        block = line.at[t % SLOTS, owner, rows, :]
+        return pltpu.make_async_remote_copy(
+            src_ref=block, dst_ref=block, send_sem=line_s.at[t, i], recv_sem=line_r.at[t, i],
+            device_id=on_expert(expert_at((up, dn, up, dn)[i])), device_id_type=MESH)
+
+    def open_line(t):
+        place = ends(t)[0]
+        whole = line.at[t % SLOTS, place]
+        pltpu.make_async_copy(whole, whole, fill_sem.at[t]).wait()
+        if t >= SLOTS:
+            pl.semaphore_wait(free.at[t - SLOTS], 2)
+        line_copy(t, 0).start()
+        line_copy(t, 1).start()
+
+    def pass_line(t):
+        line_copy(t, 0).wait_recv()
+        line_copy(t, 2).start()
+        line_copy(t, 1).wait_recv()
+        line_copy(t, 3).start()
+
+    def info_copy(a, d):
+        place, expert_at = ends(a)
+        there = lax.rem(place + d, LINE)
+        return pltpu.make_async_remote_copy(
+            src_ref=weigh.at[there] if a == 0 else weigh.at[:, there], dst_ref=pick_ref.at[a, 1, place],
+            send_sem=info_s.at[a, d], recv_sem=info_r.at[a, d],
+            device_id=on_expert(expert_at(there)), device_id_type=MESH)
+
+    def column(values):
+        owner = lax.broadcasted_iota(jnp.int32, (ROWS, EXP), 0) // CAP
+        spread = (owner == lax.broadcasted_iota(jnp.int32, (ROWS, EXP), 1)).astype(BF)
+        table = contract(spread, values.astype(BF), ((1,), (0,)))
+        slot = lax.rem(lax.broadcasted_iota(jnp.int32, (ROWS, CAP), 0), CAP)
+        return jnp.sum(jnp.where(slot == lax.broadcasted_iota(jnp.int32, (ROWS, CAP), 1), table, 0.0),
+                       axis=1, keepdims=True)
+
+    def live_mask():
+        own = lax.broadcasted_iota(jnp.int32, (EXP, EXP), 0) == lax.broadcasted_iota(jnp.int32, (EXP, EXP), 1)
+        count = jnp.sum(jnp.where(own, jnp.broadcast_to(count_ref[...].astype(F32), (EXP, EXP)), 0.0),
+                        axis=1, keepdims=True)
+        return lax.broadcasted_iota(jnp.int32, (EXP, CAP), 1).astype(F32) < count
+
+    def describe():
+        token = column(jnp.where(live_mask(), index_ref[0].astype(F32), -1.0))
+        prob = column(prob_ref[0])
+        hit = token == lax.broadcasted_iota(jnp.int32, (ROWS, TOK), 1).astype(F32)
+        rows = jnp.where(hit, jnp.broadcast_to(prob, (ROWS, TOK)), 0.0).astype(BF)
+        weigh[...] = rows.reshape(LINE, LINE, CAP, TOK)
+
+    def select(a):
+        for d in range(1, LINE):
+            info_copy(a, d).wait_recv()
+        for q in range(LINE):
+            pick_ref[a, 0, q] = jnp.where(pick_ref[a, 1, q].astype(F32) > 0.0, 1.0, 0.0).astype(BF)
+
+    def selector():
+        hit = weigh[...].reshape(ROWS, TOK).astype(F32) > 0.0
+        place_ref[...] = jnp.where(hit, 1.0, 0.0).astype(BF).T
+
+    def pick_rows(t):
+        line_copy(t, 2).wait_recv()
+        line_copy(t, 3).wait_recv()
+        if t >= SEND:
+            for d in range(1, LINE):
+                disp_copy(t - SEND, d).wait_send()
+        kind = 0 if t < 2 * NCH else 1
+        for q in range(LINE):
+            rows = contract(pick_ref[t % 2, kind, q].reshape(LINE * CAP, TOK), line[t % SLOTS, q], ((1,), (0,)))
+            send[t % SEND, :, q] = rows.astype(BF).reshape(LINE, CAP, HALF)
+        disp_local(t).start()
+        for d in range(1, LINE):
+            disp_copy(t, d).start()
+        if t + SLOTS < STEPS:
+            place, expert_at = ends(t)
+            line_copy(t, 2).wait_send()
+            line_copy(t, 3).wait_send()
+            for q in (lax.rem(place + 1, LINE), lax.rem(place + 3, LINE)):
+                pl.semaphore_signal(free.at[t], inc=1, device_id=on_expert(expert_at(q)), device_id_type=MESH)
+            line_copy(t, 0).wait_send()
+            line_copy(t, 1).wait_send()
+            fill(t + SLOTS)
 
     def landing(t):
-        return (got_x if t < NCH else got_y).at[t % NCH]
-
-    def disp_copy(t, k):
+        buffer = (got_x if t < 2 * NCH else got_y).at[(t // 2) % NCH]
+        cols = pl.ds((t % 2) * HALF, HALF)
+        return buffer.at[:, z, :, cols] if t % 2 == 0 else buffer.at[x, :, :, cols]
+
+    def disp_copy(t, d):
+        place, expert_at = ends(t + 1)
+        there = lax.rem(place + d, LINE)
         return pltpu.make_async_remote_copy(
-            src_ref=send.at[t % SEND, peer(k)], dst_ref=landing(t).at[me],
-            send_sem=disp_s.at[t, k], recv_sem=disp_r.at[t, k],
-            device_id=on_expert(peer(k)), device_id_type=MESH)
+            src_ref=send.at[t % SEND, there], dst_ref=landing(t),
+            send_sem=disp_s.at[t, d], recv_sem=disp_r.at[t, d],
+            device_id=on_expert(expert_at(there)), device_id_type=MESH)
 
     def disp_local(t):
-        return pltpu.make_async_copy(send.at[t % SEND, me], landing(t).at[me], disp_l.at[t])
-
-    def disp_start(t):
-        each_peer(lambda k: disp_copy(t, k).start())
-        disp_local(t).start()
-
-    def disp_sent(t):
-        each_peer(lambda k: disp_copy(t, k).wait_send())
+        return pltpu.make_async_copy(send.at[t % SEND, ends(t + 1)[0]], landing(t), disp_l.at[t])
 
     def disp_wait(t):
         disp_local(t).wait()
-        each_peer(lambda k: disp_copy(t, k).wait_recv())
+        for d in range(1, LINE):
+            disp_copy(t, d).wait_recv()
 
     def unit(u):
         if u < NCH:
@@ -135,7 +221,7 @@
     def product(u, core_half, write):
         rows, right, col = unit(u)
         start = pl.multiple_of(core_half * HALF, HALF)
-        lhs_t[...] = rows[:, :, pl.ds(start, HALF)].reshape(ROWS, HALF).T
+        lhs_t[...] = rows[:, :, :, pl.ds(start, HALF)].reshape(ROWS, HALF).T
         for n in range(3):
             cols = slice(n * 256, (n + 1) * 256)
             write(cols, contract(lhs_t[...], right[:, col + n * 256:col + (n + 1) * 256], ((1,), (0,))))
@@ -216,7 +302,8 @@
             stage3(t - 3)
 
     def forward(c):
-        disp_wait(c)
+        disp_wait(2 * c)
+        disp_wait(2 * c + 1)
         wait_gu(c % NWGU)
 
         def step(n, carry):
@@ -244,8 +331,13 @@
 
         lax.fori_loop(0, EXP, step, 0)
 
+    def landed(c):
+        disp_wait(2 * (NCH + c))
+        disp_wait(2 * (NCH + c) + 1)
+
     def backward(c):
-        disp_wait(NCH + c)
+        if c < NCH - 1:
+            landed(c)
         wait_dn(c % NWD)
         rows = got_y[c].reshape(ROWS, W)
         for n in range(3):
@@ -280,18 +372,18 @@
 
     def back_copy(c, k):
         return pltpu.make_async_remote_copy(
-            src_ref=got_y.at[c, peer(k)], dst_ref=got_back.at[c, me], send_sem=back_s.at[c, k],
+            src_ref=got_y.at[c, lax.rem(x + k // 4, 4), lax.rem(z + lax.rem(k, 4), 4)], dst_ref=got_back.at[c, me], send_sem=back_s.at[c, k],
             recv_sem=back_r.at[c, k], device_id=on_expert(peer(k)), device_id_type=MESH)
 
     def back_local(c):
-        return pltpu.make_async_copy(got_y.at[c, me], got_back.at[c, me], back_l.at[c])
+        return pltpu.make_async_copy(got_y.at[c, x, z], got_back.at[c, me], back_l.at[c])
 
     def give_back(c):
         wait_gu(c % NWGU)
         for n in range(W // 256):
             cols = slice(n * 256, (n + 1) * 256)
             part = contract(grads[...], wgu[c % NWGU, cols, :], ((1,), (1,)))
-            got_y[c, :, :, cols] = part.astype(BF).reshape(EXP, CAP, 256)
+            got_y[c, :, :, :, cols] = part.astype(BF).reshape(LINE, LINE, CAP, 256)
         each_peer(lambda k: back_copy(c, k).start())
         back_local(c).start()
         if c + NWGU < NCH:
@@ -307,47 +399,108 @@
                 f = feature(c, 4 * h + b)
                 tg_ref[:, f:f + PIECE] = part[:, b * PIECE:(b + 1) * PIECE]
 
-    gather(0)
-    gather(1)
+    def store(i, src, dst):
+        return pltpu.make_async_copy(src, dst, out_sem.at[i])
+
+    for t in range(SLOTS):
+        fill(t)
+    describe()
+    pick_ref[0, 1, x] = weigh[x]
+    pick_ref[1, 1, z] = weigh[:, z]
     pl.semaphore_wait(barrier, EXP - 1 + 3)
-    disp_start(0)
-    disp_start(1)
-    gather(2)
-    disp_start(2)
-    for t in range(2 * NCH):
-        if t < NCH:
-            forward(t)
-        if t == NCH - 1:
+    open_line(0)
+    open_line(1)
+    for a in range(2):
+        for d in range(1, LINE):
+            info_copy(a, d).start()
+    for t in range(2, 4):
+        open_line(t)
+    pass_line(0)
+    pass_line(1)
+    select(0)
+    open_line(4)
+    pick_rows(0)
+    select(1)
+    open_line(5)
+    pick_rows(1)
+    load_gu(0, 0)
+    pass_line(2)
+    open_line(6)
+    pass_line(3)
+    load_gu(1, 1)
+    pass_line(4)
+    for c in range(NWD):
+        load_dn(c, c)
+    for t in range(STEPS):
+        if t + PASS < STEPS:
+            pass_line(t + PASS)
+        if t + OPEN < STEPS:
+            open_line(t + OPEN)
+        if t + PICK < STEPS:
+            pick_rows(t + PICK)
+        c = t // 2
+        if t % 2 == 1:
+            if c < NCH:
+                forward(c)
+            else:
+                if t == STEPS - 1:
+                    landed(NCH - 1)
+                    stage0(NCH - 1)
+                backward(c - NCH)
+        if t == 2:
+            selector()
+        if t == 2 * NCH - 1:
             activate()
-        if t >= NCH:
-            backward(t - NCH)
-        if t + SEND < 2 * NCH:
-            disp_sent(t)
-            gather(t + SEND)
-            disp_start(t + SEND)
-        if t >= NCH:
-            tick(t - NCH)
+        u = c - NCH
+        if 0 <= u < NCH - 1 and t % 2 == 1:
+            stage0(u)
+            if u >= 2:
+                stage3(u - 2)
+        if 1 <= u and t % 2 == 0:
+            stage1(u - 1)
+            if u >= 2:
+                stage2(u - 2)
     differentiate()
-    each_peer(lambda k: route_copy(k).start())
-    route_local().start()
-    last = UNITS + 3
-    for t in range(NCH, last):
-        tick(t)
+    for t in range(NCH, UNITS + 3):
+        stage1(t - 1) if t - 1 < UNITS else None
+        stage0(t) if t < UNITS else None
+        if NCH - 2 <= t - 2 < UNITS:
+            stage2(t - 2)
+        if t == NCH:
+            stage3(NCH - 3)
         r = t - NCH
         if r < NCH:
             give_back(r)
+        if r == NCH:
+            each_peer(lambda k: route_copy(k).start())
+            route_local().start()
+        if NCH - 2 <= t - 3:
+            stage3(t - 3)
+        if r == 2:
+            store(0, gd_ref, gd_hbm).start()
         if r >= 3 and r % 2 == 1 and (r - 3) // 2 < NCH:
             combine((r - 3) // 2)
+        if t == UNITS + 1:
+            store(1, gg_ref, gg_hbm).start()
+            store(3, tg_ref, tg_hbm).start()
+    store(2, gu_ref, gu_hbm).start()
     route_local().wait()
     each_peer(lambda k: route_copy(k).wait_recv())
     lane = lax.broadcasted_iota(jnp.int32, (EXP, CAP, 128), 2)
     slot = lax.broadcasted_iota(jnp.int32, (EXP, CAP, 128), 1)
     dots = jnp.sum(jnp.where(lane == slot, got_r[...], 0.0), axis=1)[:, :CAP]
-    prob = prob_ref[...].astype(F32)
-    live = prob > 0.0
-    route_ref[...] = jnp.where(live, dots / jnp.where(live, prob, 1.0), 0.0).astype(BF)
-    for t in range(2 * NCH - SEND, 2 * NCH):
-        disp_sent(t)
+    prob = prob_ref[0].astype(F32)
+    live = live_mask()
+    route_ref[0] = jnp.where(live, dots / jnp.where(live, prob, 1.0), 0.0).astype(BF)
+    for a in range(2):
+        for d in range(1, LINE):
+            info_copy(a, d).wait_send()
+    for t in range(STEPS - SLOTS, STEPS):
+        for i in range(4):
+            line_copy(t, i).wait_send()
+    for t in range(STEPS - SEND, STEPS):
+        for d in range(1, LINE):
+            disp_copy(t, d).wait_send()
     for c in range(NCH):
         each_peer(lambda k: back_copy(c, k).wait_send())
     each_peer(lambda k: route_copy(k).wait_send())
@@ -356,35 +509,49 @@
     for u in range(UNITS - 3, UNITS):
         for i in range(6):
             ring_copy(u, i).wait_send()
+    for i, (src, dst) in enumerate(((gd_ref, gd_hbm), (gg_ref, gg_hbm), (gu_ref, gu_hbm), (tg_ref, tg_hbm))):
+        store(i, src, dst).wait()
+
+
+def finish(*refs):
+    sources, results, held, sems = refs[:5], refs[5:10], refs[10:15], refs[15]
+    loads = [pltpu.make_async_copy(a, b, sems.at[0, i]) for i, (a, b) in enumerate(zip(sources, held))]
+    stores = [pltpu.make_async_copy(a, b, sems.at[1, i]) for i, (a, b) in enumerate(zip(held, results))]
+    for copy in loads:
+        copy.start()
+    for i in (1, 2, 3, 4, 0):
+        loads[i].wait()
+        stores[i].start()
+    for copy in stores:
+        copy.wait()
 
 
 def shards(tokens, out_grad, group_token, group_count, group_prob, w_gate, w_up, w_down):
-    index, prob = group_token[0], group_prob[0]
-    live = lax.broadcasted_iota(jnp.int32, (EXP, CAP), 1) < group_count[0][:, None]
-    index = jnp.where(live, index, -1).reshape(ROWS)
-    prob = jnp.where(live, prob, jnp.zeros((), BF))
-    hit = index[:, None] == lax.broadcasted_iota(jnp.int32, (ROWS, TOK), 1)
-    pick = hit.astype(BF)
-    pick_prob = jnp.where(hit, prob.reshape(ROWS)[:, None], jnp.zeros((), BF))
-    place = (index[None, :] == lax.broadcasted_iota(jnp.int32, (TOK, ROWS), 0)).astype(BF)
     vmem = pl.BlockSpec(memory_space=pltpu.VMEM)
     hbm = pl.BlockSpec(memory_space=pl.ANY)
     dma = pltpu.SemaphoreType.DMA
-    token_grad, route_grad, grad_gate, grad_up, grad_down = pl.pallas_call(
+    results = pl.pallas_call(
         body,
         out_shape=(
             jax.ShapeDtypeStruct((TOK, D), BF),
-            jax.ShapeDtypeStruct((EXP, CAP), BF),
+            jax.ShapeDtypeStruct((1, EXP, CAP), BF),
             jax.ShapeDtypeStruct((D // 8, FF), BF),
             jax.ShapeDtypeStruct((D // 8, FF), BF),
             jax.ShapeDtypeStruct((FF, D // 8), BF),
         ),
-        in_specs=[vmem] * 6 + [hbm] * 3,
-        out_specs=[vmem] * 5,
+        in_specs=[vmem] * 3 + [hbm] * 5,
+        out_specs=[hbm, vmem, hbm, hbm, hbm],
         scratch_shapes=[
-            pltpu.VMEM((SEND, EXP, CAP, W), BF),
-            pltpu.VMEM((NCH, EXP, CAP, W), BF),
-            pltpu.VMEM((NCH, EXP, CAP, W), BF),
+            pltpu.VMEM((2, 2, LINE, LINE, CAP, TOK), BF),
+            pltpu.VMEM((TOK, ROWS), BF),
+            pltpu.VMEM((TOK, D), BF),
+            pltpu.VMEM((D // 8, FF), BF), pltpu.VMEM((D // 8, FF), BF), pltpu.VMEM((FF, D // 8), BF),
+            dma((4,)),
+            pltpu.VMEM((LINE, LINE, CAP, TOK), BF),
+            pltpu.VMEM((SLOTS, LINE, TOK, HALF), BF),
+            pltpu.VMEM((SEND, LINE, LINE, CAP, HALF), BF),
+            pltpu.VMEM((NCH, LINE, LINE, CAP, W), BF),
+            pltpu.VMEM((NCH, LINE, LINE, CAP, W), BF),
             pltpu.VMEM((NWGU, W, 2 * FF), BF),
             pltpu.VMEM((NWD, FF, W), BF),
             pltpu.VMEM((ROWS, 2 * FF), F32),
@@ -402,7 +569,9 @@
             pltpu.VMEM((UNITS, 2, PIECE // 2, FF), BF),
             pltpu.VMEM((UNITS, 2, PIECE // 2, FF), BF),
             pltpu.VMEM((UNITS, 2, PIECE // 2, FF), BF),
-            dma((2 * NCH, EXP)), dma((2 * NCH, EXP)), dma((2 * NCH,)),
+            dma((2, LINE)), dma((2, LINE)), dma((STEPS,)), dma((STEPS, 4)), dma((STEPS, 4)),
+            pltpu.SemaphoreType.REGULAR((SLOTS,)),
+            dma((STEPS, LINE)), dma((STEPS, LINE)), dma((STEPS,)),
             dma((NCH, EXP)), dma((NCH, EXP)), dma((NCH,)),
             dma((EXP,)), dma((EXP,)), dma((1,)),
             dma((NWGU,)), dma((NWD,)),
@@ -411,8 +580,16 @@
         compiler_params=pltpu.CompilerParams(
             collective_id=0, has_side_effects=True, vmem_limit_bytes=64 << 20),
         cost_estimate=pl.CostEstimate(flops=8 * 2 * ROWS * D * FF, bytes_accessed=40 << 20, transcendentals=ROWS * FF),
-    )(pick, pick_prob, place, prob, tokens, out_grad, w_gate[0], w_up[0], w_down[0])
-    return token_grad, route_grad[None], grad_gate[None], grad_up[None], grad_down[None]
+    )(group_token, group_count, group_prob, tokens, out_grad, w_gate[0], w_up[0], w_down[0])
+    token_grad, route_grad, grad_gate, grad_up, grad_down = pl.pallas_call(
+        finish,
+        out_shape=tuple(jax.ShapeDtypeStruct(r.shape, r.dtype) for r in results),
+        in_specs=[hbm] * 5,
+        out_specs=[hbm] * 5,
+        scratch_shapes=[pltpu.VMEM(r.shape, r.dtype) for r in results] + [dma((2, 5))],
+        compiler_params=pltpu.CompilerParams(vmem_limit_bytes=60 << 20),
+    )(*results)
+    return token_grad, route_grad, grad_gate[None], grad_up[None], grad_down[None]
 
 
 def solution(mesh):

time: 196 us -> 175 us (0.89)
  local copies, waits for them, and re-layouts: 11.4 us -> 0 us
  Pallas kernels: 179 us -> 173 us
  other arithmetic: 4.42 us -> 0 us
    unnamed x5 -> x0, local copies, waits for them, and re-layouts: 9.74 us -> none
    pallas_call x1, Pallas kernels: 179 us -> 170 us  [shards(): pl.pallas_call(body, out_shape=(jax.ShapeDtypeStruct((TOK, D), BF), jax.S...]
    pallas_call x0 -> x1, Pallas kernels: none -> 3.29 us  [shards(): pl.pallas_call(finish, out_shape=tuple((jax.ShapeDtypeStruct(r.shape, r.d...]
    select_n x4 -> x0, other arithmetic: 2.23 us -> none  [the longest x2 1.36 us: shards(): prob = jnp.where(live, prob, jnp.zeros((), BF))]
where the time goes in v2:
time: 175 us; the launch traced here: 174 us
  Pallas kernels  173 us (99%)
    pallas_call x1, Pallas kernels, shards(): pl.pallas_call(body, out_shape=(jax.ShapeDtypeStruct((TOK, D), BF), jax.S...  170 us

profile of v2, /device:TPU:1, one launch (start us, length us, event | category | flops | bytes accessed | tf_op | source)
XLA Modules:
  0.0 174.3 jit_solution(3436860258248770545)
XLA Ops:
  0.6 170.2 %shard_map.119 = (bf16[128,4096]{1,0:T(8,128)(2,1)}, bf16[1,16,32]{2,1,0:T(8,128)(2,1)}, bf16[512,768]{1,0:T(8,128)(2,1)}, bf16[512,768]{1,0:T(8,128)(2,1)}, bf16[768,512]{1,0:T(8,128)(2,1)}) custom-call(s32[1,16,32]{2,1,0:T(8,128)} %index_ref.1, s32[1,16]{1,0:T(1,128)} %count_ref.1, bf16[1,16,32]{2,1,0:T(8,128)(2,1)} %prob_ref.1, ...), custom_call_target="tpu_custom_call" | custom-call | flops 25769803776 | bytes 41943040 | tf_op jit(solution)/shard_map/pallas_call | solution.py:533
  170.8 3.3 %shard_map.120 = (bf16[128,4096]{1,0:T(8,128)(2,1)}, bf16[1,16,32]{2,1,0:T(8,128)(2,1)}, bf16[512,768]{1,0:T(8,128)(2,1)}, bf16[512,768]{1,0:T(8,128)(2,1)}, bf16[768,512]{1,0:T(8,128)(2,1)}) custom-call(bf16[128,4096]{1,0:T(8,128)(2,1)} %get-tuple-element.15.refs_0_, bf16[1,16,32]{2,1,0:T(8,128)(2,1)} %get-tuple-element.16.refs_1_, ...), custom_call_target="tpu_custom_call" | custom-call | tf_op jit(solution)/shard_map/pallas_call | solution.py:584

commit v3 on v2

--- a/solution.py
+++ b/solution.py
@@ -37,11 +37,11 @@
 
 
 def body(
-    index_ref, count_ref, prob_ref, tok_hbm, dy_hbm, wg_hbm, wu_hbm, wd_hbm,
-    tg_hbm, route_ref, gg_hbm, gu_hbm, gd_hbm,
-    pick_ref, place_ref, tg_ref, gg_ref, gu_ref, gd_ref, out_sem, weigh, line, send, got_x, got_y, wgu, wdn, acc, hgrad, hidden, grads, got_back, rbuf, got_r,
+    index_hbm, count_hbm, prob_hbm, tok_hbm, dy_hbm, wg_hbm, wu_hbm, wd_hbm,
+    tg_hbm, route_hbm, gg_hbm, gu_hbm, gd_hbm,
+    index_ref, count_ref, prob_ref, route_ref, in_sem, pick_ref, place_ref, tg_ref, gg_ref, gu_ref, gd_ref, out_sem, weigh, line, send, got_x, got_y, wgu, wdn, acc, hgrad, hidden, grads, got_back, rbuf, got_r,
     lhs_t, own, mate_out, mate_in, total, far, near, relay,
-    info_s, info_r, fill_sem, line_s, line_r, free, disp_s, disp_r, disp_l, back_s, back_r, back_l, rs_s, rs_r, rs_l, wgu_sem, wdn_sem,
+    info_s, info_r, fill_sem, line_s, line_r, free, disp_s, disp_r, back_s, back_r, rs_s, rs_r, wgu_sem, wdn_sem,
     mate_s, mate_r, ring_s, ring_r,
 ):
     dp = lax.axis_index("dp")
@@ -65,6 +65,9 @@
             return carry
         lax.fori_loop(0, EXP - 1, step, 0)
 
+    def wait_bytes(like, sem):
+        pltpu.make_async_copy(like, like, sem).wait()
+
     def load_gu(chunk, slot):
         for b in range(8):
             rows = pl.ds(feature(chunk, b), PIECE)
@@ -102,7 +105,7 @@
         for b in range(4):
             pltpu.make_async_copy(
                 source.at[:, pl.ds(feature((t // 2) % NCH, 4 * (t % 2) + b), PIECE)],
-                line.at[t % SLOTS, place, :, pl.ds(b * PIECE, PIECE)], fill_sem.at[t]).start()
+                line.at[t % SLOTS, place, :, pl.ds(b * PIECE, PIECE)], fill_sem.at[t % SLOTS]).start()
 
     def line_copy(t, i):
         place, expert_at = ends(t)
@@ -111,13 +114,16 @@
         rows = (pl.ds(0, TOK), pl.ds(0, TOK), pl.ds(0, TOK // 2), pl.ds(TOK // 2, TOK // 2))[i]
         block = line.at[t % SLOTS, owner, rows, :]
         return pltpu.make_async_remote_copy(
-            src_ref=block, dst_ref=block, send_sem=line_s.at[t, i], recv_sem=line_r.at[t, i],
+            src_ref=block, dst_ref=block, send_sem=line_s.at[t % SLOTS], recv_sem=line_r.at[t % SLOTS, min(i, 2)],
             device_id=on_expert(expert_at((up, dn, up, dn)[i])), device_id_type=MESH)
+
+    def line_sent(t):
+        wait_bytes(line.at[t % SLOTS, pl.ds(0, 3)], line_s.at[t % SLOTS])
 
     def open_line(t):
         place = ends(t)[0]
         whole = line.at[t % SLOTS, place]
-        pltpu.make_async_copy(whole, whole, fill_sem.at[t]).wait()
+        pltpu.make_async_copy(whole, whole, fill_sem.at[t % SLOTS]).wait()
         if t >= SLOTS:
             pl.semaphore_wait(free.at[t - SLOTS], 2)
         line_copy(t, 0).start()
@@ -134,7 +140,7 @@
         there = lax.rem(place + d, LINE)
         return pltpu.make_async_remote_copy(
             src_ref=weigh.at[there] if a == 0 else weigh.at[:, there], dst_ref=pick_ref.at[a, 1, place],
-            send_sem=info_s.at[a, d], recv_sem=info_r.at[a, d],
+            send_sem=info_s.at[a], recv_sem=info_r.at[a],
             device_id=on_expert(expert_at(there)), device_id_type=MESH)
 
     def column(values):
@@ -159,8 +165,7 @@
         weigh[...] = rows.reshape(LINE, LINE, CAP, TOK)
 
     def select(a):
-        for d in range(1, LINE):
-            info_copy(a, d).wait_recv()
+        wait_bytes(weigh.at[pl.ds(0, 3)], info_r.at[a])
         for q in range(LINE):
             pick_ref[a, 0, q] = jnp.where(pick_ref[a, 1, q].astype(F32) > 0.0, 1.0, 0.0).astype(BF)
 
@@ -169,11 +174,9 @@
         place_ref[...] = jnp.where(hit, 1.0, 0.0).astype(BF).T
 
     def pick_rows(t):
-        line_copy(t, 2).wait_recv()
-        line_copy(t, 3).wait_recv()
+        wait_bytes(line.at[t % SLOTS, 0], line_r.at[t % SLOTS, 2])
         if t >= SEND:
-            for d in range(1, LINE):
-                disp_copy(t - SEND, d).wait_send()
+            disp_sent(t - SEND)
         kind = 0 if t < 2 * NCH else 1
         for q in range(LINE):
             rows = contract(pick_ref[t % 2, kind, q].reshape(LINE * CAP, TOK), line[t % SLOTS, q], ((1,), (0,)))
@@ -183,12 +186,9 @@
             disp_copy(t, d).start()
         if t + SLOTS < STEPS:
             place, expert_at = ends(t)
-            line_copy(t, 2).wait_send()
-            line_copy(t, 3).wait_send()
+            line_sent(t)
             for q in (lax.rem(place + 1, LINE), lax.rem(place + 3, LINE)):
                 pl.semaphore_signal(free.at[t], inc=1, device_id=on_expert(expert_at(q)), device_id_type=MESH)
-            line_copy(t, 0).wait_send()
-            line_copy(t, 1).wait_send()
             fill(t + SLOTS)
 
     def landing(t):
@@ -201,16 +201,18 @@
         there = lax.rem(place + d, LINE)
         return pltpu.make_async_remote_copy(
             src_ref=send.at[t % SEND, there], dst_ref=landing(t),
-            send_sem=disp_s.at[t, d], recv_sem=disp_r.at[t, d],
+            send_sem=disp_s.at[t % SEND], recv_sem=disp_r.at[t],
             device_id=on_expert(expert_at(there)), device_id_type=MESH)
 
     def disp_local(t):
-        return pltpu.make_async_copy(send.at[t % SEND, ends(t + 1)[0]], landing(t), disp_l.at[t])
+        return pltpu.make_async_copy(send.at[t % SEND, ends(t + 1)[0]], landing(t), disp_r.at[t])
+
+    def disp_sent(t):
+        wait_bytes(send.at[t % SEND, pl.ds(0, 3)], disp_s.at[t % SEND])
 
     def disp_wait(t):
-        disp_local(t).wait()
-        for d in range(1, LINE):
-            disp_copy(t, d).wait_recv()
+        buffer = (got_x if t < 2 * NCH else got_y).at[(t // 2) % NCH]
+        wait_bytes(buffer.at[:, :, :, pl.ds((t % 2) * HALF, HALF)], disp_r.at[t])
 
     def unit(u):
         if u < NCH:
@@ -228,7 +230,7 @@
 
     def mate_copy(u):
         return pltpu.make_async_remote_copy(
-            src_ref=mate_out.at[u % 2], dst_ref=mate_in.at[u], send_sem=mate_s.at[u], recv_sem=mate_r.at[u],
+            src_ref=mate_out.at[u % 2], dst_ref=mate_in.at[u], send_sem=mate_s.at[u % 2], recv_sem=mate_r.at[u],
             device_id=mate, device_id_type=MESH)
 
     def ring_copy(u, i):
@@ -238,8 +240,11 @@
         part = (lower, upper)[(way, 1 - way, way)[kind]]
         return pltpu.make_async_remote_copy(
             src_ref=total.at[u % 3, owner, part, :], dst_ref=(far, near, relay)[kind].at[u, way],
-            send_sem=ring_s.at[u, i], recv_sem=ring_r.at[u, i],
+            send_sem=ring_s.at[u % 3], recv_sem=ring_r.at[u, min(i, 2)],
             device_id=side[way], device_id_type=MESH)
+
+    def ring_sent(u):
+        wait_bytes(total.at[u % 3, pl.ds(0, 3)], ring_s.at[u % 3])
 
     def stage0(u):
         if u >= 2:
@@ -257,8 +262,7 @@
 
     def stage1(u):
         if u >= 3:
-            for i in range(6):
-                ring_copy(u - 3, i).wait_send()
+            ring_sent(u - 3)
         mate_copy(u).wait_recv()
         for q in range(4):
             rows = slice(q * PIECE, (q + 1) * PIECE)
@@ -277,8 +281,7 @@
 
     def stage3(u):
         half = PIECE // 2
-        for i in range(2, 6):
-            ring_copy(u, i).wait_recv()
+        wait_bytes(total.at[0, pl.ds(0, 2)], ring_r.at[u, 2])
         halves = []
         for h in range(2):
             rows = slice(h * half, (h + 1) * half)
@@ -352,11 +355,11 @@
 
     def route_copy(k):
         return pltpu.make_async_remote_copy(
-            src_ref=rbuf.at[peer(k)], dst_ref=got_r.at[me], send_sem=rs_s.at[k], recv_sem=rs_r.at[k],
+            src_ref=rbuf.at[peer(k)], dst_ref=got_r.at[me], send_sem=rs_s.at[0], recv_sem=rs_r.at[0],
             device_id=on_expert(peer(k)), device_id_type=MESH)
 
     def route_local():
-        return pltpu.make_async_copy(rbuf.at[me], got_r.at[me], rs_l.at[0])
+        return pltpu.make_async_copy(rbuf.at[me], got_r.at[me], rs_r.at[0])
 
     def differentiate():
         def step(i, carry):
@@ -372,11 +375,11 @@
 
     def back_copy(c, k):
         return pltpu.make_async_remote_copy(
-            src_ref=got_y.at[c, lax.rem(x + k // 4, 4), lax.rem(z + lax.rem(k, 4), 4)], dst_ref=got_back.at[c, me], send_sem=back_s.at[c, k],
-            recv_sem=back_r.at[c, k], device_id=on_expert(peer(k)), device_id_type=MESH)
+            src_ref=got_y.at[c, lax.rem(x + k // 4, 4), lax.rem(z + lax.rem(k, 4), 4)], dst_ref=got_back.at[c, me], send_sem=back_s.at[c],
+            recv_sem=back_r.at[c], device_id=on_expert(peer(k)), device_id_type=MESH)
 
     def back_local(c):
-        return pltpu.make_async_copy(got_y.at[c, x, z], got_back.at[c, me], back_l.at[c])
+        return pltpu.make_async_copy(got_y.at[c, x, z], got_back.at[c, me], back_r.at[c])
 
     def give_back(c):
         wait_gu(c % NWGU)
@@ -390,8 +393,7 @@
             load_gu(c + NWGU, c % NWGU)
 
     def combine(c):
-        back_local(c).wait()
-        each_peer(lambda k: back_copy(c, k).wait_recv())
+        wait_bytes(got_back.at[c], back_r.at[c])
         for h in range(2):
             rows = got_back[c, :, :, h * HALF:(h + 1) * HALF].reshape(ROWS, HALF)
             part = contract(place_ref[...], rows, ((1,), (0,))).astype(BF)
@@ -402,8 +404,14 @@
     def store(i, src, dst):
         return pltpu.make_async_copy(src, dst, out_sem.at[i])
 
+    small = [pltpu.make_async_copy(a, b, in_sem.at[i]) for i, (a, b) in enumerate(
+        ((index_hbm, index_ref), (count_hbm, count_ref), (prob_hbm, prob_ref)))]
+    for copy in small:
+        copy.start()
     for t in range(SLOTS):
         fill(t)
+    for copy in small:
+        copy.wait()
     describe()
     pick_ref[0, 1, x] = weigh[x]
     pick_ref[1, 1, z] = weigh[:, z]
@@ -480,36 +488,34 @@
             store(0, gd_ref, gd_hbm).start()
         if r >= 3 and r % 2 == 1 and (r - 3) // 2 < NCH:
             combine((r - 3) // 2)
+        if t == UNITS:
+            wait_bytes(got_r, rs_r.at[0])
+            lane = lax.broadcasted_iota(jnp.int32, (EXP, CAP, 128), 2)
+            slot = lax.broadcasted_iota(jnp.int32, (EXP, CAP, 128), 1)
+            dots = jnp.sum(jnp.where(lane == slot, got_r[...], 0.0), axis=1)[:, :CAP]
+            prob = prob_ref[0].astype(F32)
+            live = live_mask()
+            route_ref[0] = jnp.where(live, dots / jnp.where(live, prob, 1.0), 0.0).astype(BF)
+            store(4, route_ref, route_hbm).start()
         if t == UNITS + 1:
             store(1, gg_ref, gg_hbm).start()
             store(3, tg_ref, tg_hbm).start()
     store(2, gu_ref, gu_hbm).start()
-    route_local().wait()
-    each_peer(lambda k: route_copy(k).wait_recv())
-    lane = lax.broadcasted_iota(jnp.int32, (EXP, CAP, 128), 2)
-    slot = lax.broadcasted_iota(jnp.int32, (EXP, CAP, 128), 1)
-    dots = jnp.sum(jnp.where(lane == slot, got_r[...], 0.0), axis=1)[:, :CAP]
-    prob = prob_ref[0].astype(F32)
-    live = live_mask()
-    route_ref[0] = jnp.where(live, dots / jnp.where(live, prob, 1.0), 0.0).astype(BF)
     for a in range(2):
-        for d in range(1, LINE):
-            info_copy(a, d).wait_send()
+        wait_bytes(weigh.at[pl.ds(0, 3)], info_s.at[a])
     for t in range(STEPS - SLOTS, STEPS):
-        for i in range(4):
-            line_copy(t, i).wait_send()
+        line_sent(t)
     for t in range(STEPS - SEND, STEPS):
-        for d in range(1, LINE):
-            disp_copy(t, d).wait_send()
+        disp_sent(t)
     for c in range(NCH):
-        each_peer(lambda k: back_copy(c, k).wait_send())
-    each_peer(lambda k: route_copy(k).wait_send())
+        wait_bytes(got_back.at[c, pl.ds(0, EXP - 1)], back_s.at[c])
+    wait_bytes(got_r.at[pl.ds(0, EXP - 1)], rs_s.at[0])
     for u in range(UNITS - 2, UNITS):
         mate_copy(u).wait_send()
     for u in range(UNITS - 3, UNITS):
-        for i in range(6):
-            ring_copy(u, i).wait_send()
-    for i, (src, dst) in enumerate(((gd_ref, gd_hbm), (gg_ref, gg_hbm), (gu_ref, gu_hbm), (tg_ref, tg_hbm))):
+        ring_sent(u)
+    for i, (src, dst) in enumerate((
+            (gd_ref, gd_hbm), (gg_ref, gg_hbm), (gu_ref, gu_hbm), (tg_ref, tg_hbm), (route_ref, route_hbm))):
         store(i, src, dst).wait()
 
 
@@ -527,7 +533,6 @@
 
 
 def shards(tokens, out_grad, group_token, group_count, group_prob, w_gate, w_up, w_down):
-    vmem = pl.BlockSpec(memory_space=pltpu.VMEM)
     hbm = pl.BlockSpec(memory_space=pl.ANY)
     dma = pltpu.SemaphoreType.DMA
     results = pl.pallas_call(
@@ -539,14 +544,16 @@
             jax.ShapeDtypeStruct((D // 8, FF), BF),
             jax.ShapeDtypeStruct((FF, D // 8), BF),
         ),
-        in_specs=[vmem] * 3 + [hbm] * 5,
-        out_specs=[hbm, vmem, hbm, hbm, hbm],
+        in_specs=[hbm] * 8,
+        out_specs=[hbm] * 5,
         scratch_shapes=[
+            pltpu.VMEM((1, EXP, CAP), jnp.int32), pltpu.VMEM((1, EXP), jnp.int32),
+            pltpu.VMEM((1, EXP, CAP), BF), pltpu.VMEM((1, EXP, CAP), BF), dma((3,)),
             pltpu.VMEM((2, 2, LINE, LINE, CAP, TOK), BF),
             pltpu.VMEM((TOK, ROWS), BF),
             pltpu.VMEM((TOK, D), BF),
             pltpu.VMEM((D // 8, FF), BF), pltpu.VMEM((D // 8, FF), BF), pltpu.VMEM((FF, D // 8), BF),
-            dma((4,)),
+            dma((5,)),
             pltpu.VMEM((LINE, LINE, CAP, TOK), BF),
             pltpu.VMEM((SLOTS, LINE, TOK, HALF), BF),
             pltpu.VMEM((SEND, LINE, LINE, CAP, HALF), BF),
@@ -569,13 +576,13 @@
             pltpu.VMEM((UNITS, 2, PIECE // 2, FF), BF),
             pltpu.VMEM((UNITS, 2, PIECE // 2, FF), BF),
             pltpu.VMEM((UNITS, 2, PIECE // 2, FF), BF),
-            dma((2, LINE)), dma((2, LINE)), dma((STEPS,)), dma((STEPS, 4)), dma((STEPS, 4)),
+            dma((2,)), dma((2,)), dma((SLOTS,)), dma((SLOTS,)), dma((SLOTS, 3)),
             pltpu.SemaphoreType.REGULAR((SLOTS,)),
-            dma((STEPS, LINE)), dma((STEPS, LINE)), dma((STEPS,)),
-            dma((NCH, EXP)), dma((NCH, EXP)), dma((NCH,)),
-            dma((EXP,)), dma((EXP,)), dma((1,)),
+            dma((SEND,)), dma((STEPS,)),
+            dma((NCH,)), dma((NCH,)),
+            dma((1,)), dma((1,)),
             dma((NWGU,)), dma((NWD,)),
-            dma((UNITS,)), dma((UNITS,)), dma((UNITS, 6)), dma((UNITS, 6)),
+            dma((2,)), dma((UNITS,)), dma((3,)), dma((UNITS, 3)),
         ],
         compiler_params=pltpu.CompilerParams(
             collective_id=0, has_side_effects=True, vmem_limit_bytes=64 << 20),

time: 175 us -> 169 us (0.966)
  Pallas kernels: 173 us -> 167 us
    pallas_call x1, Pallas kernels: 170 us -> 164 us  [shards(): pl.pallas_call(body, out_shape=(jax.ShapeDtypeStruct((TOK, D), BF), jax.S...]
where the time goes in v3:
time: 169 us; the launch traced here: 168 us
  Pallas kernels  167 us (99%)
    pallas_call x1, Pallas kernels, shards(): pl.pallas_call(body, out_shape=(jax.ShapeDtypeStruct((TOK, D), BF), jax.S...  164 us

profile of v3, /device:TPU:1, one launch (start us, length us, event | category | flops | bytes accessed | tf_op | source)
XLA Modules:
  0.0 168.1 jit_solution(17559945796676551116)
XLA Ops:
  0.6 163.9 %shard_map.119 = (bf16[128,4096]{1,0:T(8,128)(2,1)}, bf16[1,16,32]{2,1,0:T(8,128)(2,1)}, bf16[512,768]{1,0:T(8,128)(2,1)}, bf16[512,768]{1,0:T(8,128)(2,1)}, bf16[768,512]{1,0:T(8,128)(2,1)}) custom-call(s32[1,16,32]{2,1,0:T(8,128)} %index_hbm.1, s32[1,16]{1,0:T(1,128)} %count_hbm.1, bf16[1,16,32]{2,1,0:T(8,128)(2,1)} %prob_hbm.1, ...), custom_call_target="tpu_custom_call" | custom-call | flops 25769803776 | bytes 41943040 | tf_op jit(solution)/shard_map/pallas_call | solution.py:538
  164.6 3.3 %shard_map.120 = (bf16[128,4096]{1,0:T(8,128)(2,1)}, bf16[1,16,32]{2,1,0:T(8,128)(2,1)}, bf16[512,768]{1,0:T(8,128)(2,1)}, bf16[512,768]{1,0:T(8,128)(2,1)}, bf16[768,512]{1,0:T(8,128)(2,1)}) custom-call(bf16[128,4096]{1,0:T(8,128)(2,1)} %get-tuple-element.15.refs_0_, bf16[1,16,32]{2,1,0:T(8,128)(2,1)} %get-tuple-element.16.refs_1_, ...), custom_call_target="tpu_custom_call" | custom-call | tf_op jit(solution)/shard_map/pallas_call | solution.py:591

commit v4 on v3

--- a/solution.py
+++ b/solution.py
@@ -92,7 +92,8 @@
     def greet(k):
         pl.semaphore_signal(barrier, inc=1, device_id=on_expert(peer(k)), device_id_type=MESH)
 
-    each_peer(greet)
+    for k in (1, 2, 3, 4, 8, 12):
+        greet(k)
     for there in (mate, side[0], side[1]):
         pl.semaphore_signal(barrier, inc=1, device_id=there, device_id_type=MESH)
 
@@ -415,7 +416,7 @@
     describe()
     pick_ref[0, 1, x] = weigh[x]
     pick_ref[1, 1, z] = weigh[:, z]
-    pl.semaphore_wait(barrier, EXP - 1 + 3)
+    pl.semaphore_wait(barrier, 6 + 3)
     open_line(0)
     open_line(1)
     for a in range(2):

time: 169 us -> 168 us (level)
  no operation moved by 1% of the time
where the time goes in v4:
time: 168 us
  Pallas kernels  167 us (99%)
    pallas_call x1, Pallas kernels, shards(): pl.pallas_call(body, out_shape=(jax.ShapeDtypeStruct((TOK, D), BF), jax.S...  164 us

profile of v4, /device:TPU:1, one launch (start us, length us, event | category | flops | bytes accessed | tf_op | source)
XLA Modules:
  0.0 168.2 jit_solution(11204869056422313929)
XLA Ops:
  0.6 164.1 %shard_map.119 = (bf16[128,4096]{1,0:T(8,128)(2,1)}, bf16[1,16,32]{2,1,0:T(8,128)(2,1)}, bf16[512,768]{1,0:T(8,128)(2,1)}, bf16[512,768]{1,0:T(8,128)(2,1)}, bf16[768,512]{1,0:T(8,128)(2,1)}) custom-call(s32[1,16,32]{2,1,0:T(8,128)} %index_hbm.1, s32[1,16]{1,0:T(1,128)} %count_hbm.1, bf16[1,16,32]{2,1,0:T(8,128)(2,1)} %prob_hbm.1, ...), custom_call_target="tpu_custom_call" | custom-call | flops 25769803776 | bytes 41943040 | tf_op jit(solution)/shard_map/pallas_call | solution.py:539
  164.7 3.3 %shard_map.120 = (bf16[128,4096]{1,0:T(8,128)(2,1)}, bf16[1,16,32]{2,1,0:T(8,128)(2,1)}, bf16[512,768]{1,0:T(8,128)(2,1)}, bf16[512,768]{1,0:T(8,128)(2,1)}, bf16[768,512]{1,0:T(8,128)(2,1)}) custom-call(bf16[128,4096]{1,0:T(8,128)(2,1)} %get-tuple-element.15.refs_0_, bf16[1,16,32]{2,1,0:T(8,128)(2,1)} %get-tuple-element.16.refs_1_, ...), custom_call_target="tpu_custom_call" | custom-call | tf_op jit(solution)/shard_map/pallas_call | solution.py:592
